TPU v7x, 256 devices: a whole 4x4x8 slice. The times are simulated.
256 devices in a mesh: prefix: 64 (over x, z, core), head: 4 (over y).
Axes of the slice: x: 4, y: 4, z: 8, core: 2. Of those that a mesh axis runs over, the one named last changes fastest.
Arguments:
- queries: bfloat16 [16384, 64, 128], P(('prefix', 'head')), may hold values from -8 to 8
- prefix_id: int32 [16384, 1], P(('prefix', 'head')), may hold values from 0 to 63; in each aligned block of 64 rows (0 to 63, 64 to 127, ...) at most 2 rows name the same one
- suffix_len: int32 [16384], P(('prefix', 'head')), may hold values from 2 to 32
- prefix_keys: bfloat16 [64, 2048, 8, 128], P('prefix', None, 'head'), may hold values from -8 to 8
- prefix_values: bfloat16 [64, 2048, 8, 128], P('prefix', None, 'head'), may hold values from -6 to 6
- suffix_keys: bfloat16 [16384, 32, 8, 128], P(('prefix', 'head')), may hold values from -8 to 8
- suffix_values: bfloat16 [16384, 32, 8, 128], P(('prefix', 'head')), may hold values from -6 to 6
- new_keys: bfloat16 [16384, 8, 128], P(('prefix', 'head')), may hold values from -8 to 8
- new_values: bfloat16 [16384, 8, 128], P(('prefix', 'head')), may hold values from -6 to 6
Outputs:
- attended: bfloat16 [16384, 64, 128], P(('prefix', 'head'))
Inputs may be any that keep to these rules, and one draw needn't show every extreme that they name: `prefix_id`: the 64 rows of one device name one prefix at most 2 times.
All inputs are finite; a program needn't handle non-finite values.
Results may differ from a plain program's by a relative error of at most 0.0036.
Values may be sent and summed in bfloat16 or wider, within the bound.
A program may use at most 64 MiB of HBM per device.

v0:
```python
import math

import jax
import jax.numpy as jnp
from jax import lax
from jax.sharding import PartitionSpec as P


def attend(received, key_cache, value_cache, scale_factor):
    lined = jnp.transpose(received, (3, 1, 0, 2, 4, 5))

    def per_head(packed_tuple):
        head_query, head_keys, head_values = packed_tuple

        def per_group(block_query_rows):
            scores = (
                jnp.einsum(
                    "ncgd,td->ncgt", block_query_rows, head_keys, preferred_element_type=jnp.float32
                )
                * scale_factor
            )
            highest = jnp.max(scores, axis=-1)
            weights_raw = jnp.exp(scores - highest[..., None])
            totals = jnp.sum(weights_raw, axis=-1)
            blended = jnp.einsum(
                "ncgt,td->ncgd",
                weights_raw.astype(jnp.bfloat16),
                head_values,
                preferred_element_type=jnp.float32,
            )
            return ((blended / totals[..., None]).astype(jnp.bfloat16), highest + jnp.log(totals))

        return lax.map(per_group, head_query)

    blended, log_mass = lax.map(
        per_head,
        (lined, jnp.transpose(key_cache, (1, 0, 2)), jnp.transpose(value_cache, (1, 0, 2))),
    )
    return (jnp.transpose(blended, (2, 1, 3, 0, 4, 5)), jnp.transpose(log_mass, (2, 1, 3, 0, 4)))


def body(
    queries,
    prefix_id,
    suffix_len,
    prefix_keys,
    prefix_values,
    suffix_keys,
    suffix_values,
    new_keys,
    new_values,
):
    row_count, head_count, head_width = queries.shape
    kv_all = suffix_keys.shape[2]
    per_kv = head_count // kv_all
    owners = lax.axis_size("prefix")
    capacity = 2 * row_count // owners
    scale_factor = 1.0 / math.sqrt(head_width)
    target = prefix_id[:, 0]
    row_index = lax.broadcasted_iota(jnp.int32, (row_count, row_count), 0)
    col_index = lax.broadcasted_iota(jnp.int32, (row_count, row_count), 1)
    earlier = (target[None, :] == target[:, None]) & (col_index < row_index)
    arrival = jnp.sum(earlier.astype(jnp.int32), axis=1)
    position = target * capacity + arrival
    query_layout = queries.reshape(row_count, kv_all, per_kv, head_width)
    outbox = (
        jnp.zeros((owners * capacity, kv_all, per_kv, head_width), jnp.bfloat16)
        .at[position]
        .set(query_layout)
    )
    outbox = outbox.reshape(owners, 1, capacity, kv_all, per_kv, head_width)
    key_cache = prefix_keys[0]
    value_cache = prefix_values[0]
    received = lax.all_to_all(
        lax.all_to_all(outbox, "prefix", split_axis=0, concat_axis=0, tiled=True),
        "head",
        split_axis=3,
        concat_axis=1,
        tiled=True,
    )
    blended, log_mass = attend(received, key_cache, value_cache, scale_factor)
    blended = lax.all_to_all(
        lax.all_to_all(blended, "prefix", split_axis=0, concat_axis=0, tiled=True),
        "head",
        split_axis=1,
        concat_axis=3,
        tiled=True,
    )
    log_mass = lax.all_to_all(
        lax.all_to_all(log_mass, "prefix", split_axis=0, concat_axis=0, tiled=True),
        "head",
        split_axis=1,
        concat_axis=3,
        tiled=True,
    )
    prefix_out = blended.reshape(owners * capacity, kv_all, per_kv, head_width)[position].astype(
        jnp.float32
    )
    prefix_mass = log_mass.reshape(owners * capacity, kv_all, per_kv)[position]
    private_scores = (
        jnp.einsum("wtfb,wmtb->wtfm", query_layout, suffix_keys, preferred_element_type=jnp.float32)
        * scale_factor
    )
    visible = (jnp.arange(suffix_keys.shape[1], dtype=jnp.int32)[None, :] < suffix_len[:, None])[
        :, None, None, :
    ]
    private_scores = jnp.where(visible, private_scores, -jnp.inf)
    own_score = (
        jnp.einsum("rkgd,rkd->rkg", query_layout, new_keys, preferred_element_type=jnp.float32)
        * scale_factor
    )
    suffix_top = jnp.maximum(jnp.max(private_scores, axis=-1), own_score)
    suffix_raw = jnp.where(visible, jnp.exp(private_scores - suffix_top[..., None]), 0.0)
    own_weight = jnp.exp(own_score - suffix_top)
    suffix_totals = jnp.sum(suffix_raw, axis=-1) + own_weight
    gathered = jnp.einsum(
        "rkgs,rskd->rkgd",
        suffix_raw.astype(jnp.bfloat16),
        suffix_values,
        preferred_element_type=jnp.float32,
    )
    gathered = (
        gathered
        + own_weight.astype(jnp.bfloat16).astype(jnp.float32)[..., None]
        * new_values.astype(jnp.float32)[:, :, None, :]
    )
    suffix_out = gathered / suffix_totals[..., None]
    suffix_mass = suffix_top + jnp.log(suffix_totals)
    ceiling = jnp.maximum(prefix_mass, suffix_mass)
    share_prefix = jnp.exp(prefix_mass - ceiling)
    share_suffix = jnp.exp(suffix_mass - ceiling)
    merged = (share_prefix[..., None] * prefix_out + share_suffix[..., None] * suffix_out) / (
        share_prefix + share_suffix
    )[..., None]
    return merged.reshape(row_count, head_count, head_width).astype(jnp.bfloat16)


def solution(mesh):
    return jax.shard_map(
        body,
        mesh=mesh,
        in_specs=(
            P(("prefix", "head"), None, None),
            P(("prefix", "head"), None),
            P(("prefix", "head")),
            P("prefix", None, "head", None),
            P("prefix", None, "head", None),
            P(("prefix", "head"), None, None, None),
            P(("prefix", "head"), None, None, None),
            P(("prefix", "head"), None, None),
            P(("prefix", "head"), None, None),
        ),
        out_specs=P(("prefix", "head"), None, None),
        check_vma=False,
    )
```

profile of v0, /device:TPU:1, one launch (start us, length us, event | category | flops | bytes accessed | tf_op | source)
XLA Modules:
  0.0 273.2 jit_solution(9314660076210602092)
XLA Ops:
  2.2 2.6 scatter_fusion
  4.8 64.0 %all_to_all.63 = bf16[64,1,2,8,8,128]{5,4,3,2,1,0:T(8,128)(2,1)S(1)} all-to-all(bf16[64,1,2,8,8,128]{5,4,3,2,1,0:T(8,128)(2,1)S(1)} %bitcast.118), channel_id=1, replica_groups=mesh['prefix'=64,'head'=4] {'prefix'}, dimensions={0} | all-to-all | bytes 4194304 | tf_op jit(solution)/shard_map/all_to_all | solution.py:75
  68.8 1.7 copy.99
  70.6 4.6 %all-to-all-start.1 = ((bf16[64,1,2,8,8,128]{5,4,2,0,1,3:T(8,128)(2,1)}), bf16[64,1,2,8,8,128]{5,4,2,0,1,3:T(8,128)(2,1)}, u32[]{:S(2)}, u32[]{:S(2)}) async-start(bf16[64,1,2,8,8,128]{5,4,2,0,1,3:T(8,128)(2,1)} %copy.99), calls=%async_computation.1 | async-start | bytes 4194304 | tf_op jit(solution)/shard_map/all_to_all | solution.py:74
  76.8 24.4 %all-to-all-done.1 = bf16[64,1,2,8,8,128]{5,4,2,0,1,3:T(8,128)(2,1)} async-done(((bf16[64,1,2,8,8,128]{5,4,2,0,1,3:T(8,128)(2,1)}), bf16[64,1,2,8,8,128]{5,4,2,0,1,3:T(8,128)(2,1)}, u32[]{:S(2)}, u32[]{:S(2)}) %all-to-all-start.1) | async-done | bytes 2097184 | tf_op jit(solution)/shard_map/all_to_all | solution.py:74
  101.2 48.3 %while.25 = (s32[]{:T(128)}, bf16[2,4,64,2,8,128]{5,4,0,3,1,2:T(8,128)(2,1)}, f32[2,4,64,2,8]{4,3,1,0,2:T(2,128)}, bf16[2,4,64,2,8,128]{5,4,3,2,0,1:T(8,128)(2,1...) while((s32[]{:T(128)}, ...), condition=%wide.region_7.8_spmd, body=%wide.region_2.7_spmd.sunk | while | flops 1090780160 | bytes 42545540 | solution.py:35
  103.1 19.9 %while.26 = (s32[]{:T(128)}, bf16[4,64,2,8,128]{4,3,2,1,0:T(8,128)(2,1)S(1)}, f32[4,64,2,8]{3,2,1,0:T(2,128)S(1)}, bf16[4,64,2,8,128]{4,3,2,1,0:T(8,128)(2,1)S(1...) while((s32[]{:T(128)}, bf16[4,64,2,8,128]{4,3,2,1,0:T(8,128)(2,1)S(1)}, ...), condition=%wide.region_6.6_spmd, body=%wide.region_3.5_spmd.sunk | while | flops 1090780160 | bytes 27078752 | solution.py:33
  104.5 1.7 fusion.71
  106.2 1.8 fusion.72
  109.5 1.7 fusion.71
  111.2 1.8 fusion.72
  114.5 1.7 fusion.71
  116.2 1.8 fusion.72
  121.2 1.8 fusion.72
  127.3 19.9 %while.26 = (s32[]{:T(128)}, bf16[4,64,2,8,128]{4,3,2,1,0:T(8,128)(2,1)S(1)}, f32[4,64,2,8]{3,2,1,0:T(2,128)S(1)}, bf16[4,64,2,8,128]{4,3,2,1,0:T(8,128)(2,1)S(1...) while((s32[]{:T(128)}, bf16[4,64,2,8,128]{4,3,2,1,0:T(8,128)(2,1)S(1)}, ...), condition=%wide.region_6.6_spmd, body=%wide.region_3.5_spmd.sunk | while | flops 1090780160 | bytes 27078752 | solution.py:33
  128.7 1.7 fusion.71
  130.4 1.8 fusion.72
  135.4 1.8 fusion.72
  140.4 1.8 fusion.72
  145.4 1.8 fusion.72
  151.4 15.6 %all_to_all.64 = f32[64,1,128]{2,1,0:T(1,128)S(1)} all-to-all(f32[64,1,128]{2,1,0:T(1,128)S(1)} %reshape.92), channel_id=1, replica_groups=mesh['prefix'=64,'head'=4] {'prefix'}, dimensions={0} | all-to-all | bytes 65536 | tf_op jit(solution)/shard_map/all_to_all | solution.py:90
  167.0 4.9 %all-to-all-start.4 = ((bf16[64,4,2,2,8,128]{5,4,3,2,1,0:T(8,128)(2,1)}), bf16[64,4,2,2,8,128]{5,4,3,2,1,0:T(8,128)(2,1)S(1)}, u32[]{:S(2)}, u32[]{:S(2)}) async-start(bf16[64,4,2,2,8,128]{5,4,3,2,1,0:T(8,128)(2,1)} %bitcast.121), calls=%async_computation.4 | async-start | bytes 4194304 | tf_op jit(solution)/shard_map/all_to_all | solution.py:83
  176.6 46.7 %all-to-all-done.4 = bf16[64,4,2,2,8,128]{5,4,3,2,1,0:T(8,128)(2,1)S(1)} async-done(((bf16[64,4,2,2,8,128]{5,4,3,2,1,0:T(8,128)(2,1)}), bf16[64,4,2,2,8,128]{5,4,3,2,1,0:T(8,128)(2,1)S(1)}, u32[]{:S(2)}, u32[]{:S(2)}) %all-to-all-start.4) | async-done | bytes 2097184 | tf_op jit(solution)/shard_map/all_to_all | solution.py:83
  223.3 3.9 %all-to-all-start.3 = ((f32[4,1,2048]{2,1,0:T(1,128)}), f32[4,1,2048]{2,1,0:T(1,128)}, u32[]{:S(2)}, u32[]{:S(2)}) async-start(f32[4,1,2048]{2,1,0:T(1,128)} %reshape.94), calls=%async_computation.3 | async-start | bytes 65536 | tf_op jit(solution)/shard_map/all_to_all | solution.py:89
  227.9 1.7 copy.115
  229.6 1.9 all-to-all-done.3
  231.5 4.6 %all-to-all-start.5 = ((bf16[64,4,2,2,8,128]{5,4,3,2,0,1:T(8,128)(2,1)}), bf16[64,4,2,2,8,128]{5,4,3,2,0,1:T(8,128)(2,1)}, u32[]{:S(2)}, u32[]{:S(2)}) async-start(bf16[64,4,2,2,8,128]{5,4,3,2,0,1:T(8,128)(2,1)} %copy.115), calls=%async_computation.5 | async-start | bytes 4194304 | tf_op jit(solution)/shard_map/all_to_all | solution.py:82
  237.0 4.6 %fusion.27 = (f32[64,8,8]{2,1,0:T(8,128)S(1)}, f32[64,8,8,32]{3,2,1,0:T(8,128)S(1)}) fusion(pred[64,32]{1,0:T(8,128)(4,1)S(1)} %iota_compare_fusion, bf16[64,32,8,128]{3,2,1,0:T(8,128)(2,1)} %param.18, bf16[64,64,128]{2,1,0:T(8,128)(2,1)S(1)} %copy-done.4), kind=kOutput, calls=%fused_computation.32 | convolution fusion | flops 33943552 | bytes 5785600 | tf_op jit(solution)/shard_map/wtfb,wmtb->wtfm/dot_general | solution.py:101
  251.8 9.0 %all-to-all-done.5 = bf16[64,4,2,2,8,128]{5,4,3,2,0,1:T(8,128)(2,1)} async-done(((bf16[64,4,2,2,8,128]{5,4,3,2,0,1:T(8,128)(2,1)}), bf16[64,4,2,2,8,128]{5,4,3,2,0,1:T(8,128)(2,1)}, u32[]{:S(2)}, u32[]{:S(2)}) %all-to-all-start.5) | async-done | bytes 2097184 | tf_op jit(solution)/shard_map/all_to_all | solution.py:82
  260.8 3.5 %copy.116 = bf16[64,4,2,2,8,128]{5,4,3,1,2,0:T(8,128)(2,1)} copy(bf16[64,4,2,2,8,128]{5,4,3,2,0,1:T(8,128)(2,1)} %all-to-all-done.5) | data formatting | bytes 4194304 | tf_op jit(solution)/shard_map/all_to_all | solution.py:82
  264.4 2.3 gather_fusion.1
  266.7 6.5 %fusion.32 = bf16[64,64,128]{2,1,0:T(8,128)(2,1)} fusion(bf16[64,32,8,128]{3,2,1,0:T(8,128)(2,1)} %param.19, bf16[64,8,8,128]{3,2,1,0:T(8,128)(2,1)S(1)} %gather_fusion.1, f32[64,8,8,32]{3,2,1,0:T(8,128)S(1)} %get-tuple-element.150, f32[64,8,8]{2,1,0:T(8,128)} %copy.121, f32[64,8,8]{2,1,0:T(8,128)} %copy.120, f32[64,8,128]{2,1,0:T(8,128)} %convert_element_type.35, ...), kind=kOutput, calls=%fused_computation.35 | convolution fusion | flops 38928384 | bytes 7178240 | tf_op jit(solution)/shard_map/rkgs,rskd->rkgd/dot_general | solution.py:116
  (103 shorter events, 49.0 us)
Async XLA Ops:
  0.0 227.2 %copy-start = (bf16[64,8,128]{2,1,0:T(8,128)(2,1)S(1)}, bf16[64,8,128]{2,1,0:T(8,128)(2,1)}, u32[]{:S(2)}) copy-start(bf16[64,8,128]{2,1,0:T(8,128)(2,1)} %param.20) | copy-start | bytes 393220
  0.0 2.1 copy-start.3
  1.6 3.2 %copy-start.11 = (s32[64]{0:T(128)}, s32[64]{0:T(128)S(1)}, u32[]{:S(2)}) copy-start(s32[64]{0:T(128)S(1)} %fusion.48) | copy-start | bytes 772
  70.6 4.6 %copy-start.5 = (bf16[1,2048,2,128]{3,2,1,0:T(2,128)(2,1)S(1)}, bf16[1,2048,2,128]{3,2,1,0:T(2,128)(2,1)}, u32[]{:S(2)}) copy-start(bf16[1,2048,2,128]{3,2,1,0:T(2,128)(2,1)} %param.17) | copy-start | bytes 3145732
  70.6 4.6 %copy-start.6 = (bf16[1,2048,2,128]{3,2,1,0:T(2,128)(2,1)S(1)}, bf16[1,2048,2,128]{3,2,1,0:T(2,128)(2,1)}, u32[]{:S(2)}) copy-start(bf16[1,2048,2,128]{3,2,1,0:T(2,128)(2,1)} %param.16) | copy-start | bytes 3145732
  70.6 30.6 %all-to-all-start.1 = ((bf16[64,1,2,8,8,128]{5,4,2,0,1,3:T(8,128)(2,1)}), bf16[64,1,2,8,8,128]{5,4,2,0,1,3:T(8,128)(2,1)}, u32[]{:S(2)}, u32[]{:S(2)}) async-start(bf16[64,1,2,8,8,128]{5,4,2,0,1,3:T(8,128)(2,1)} %copy.99), calls=%async_computation.1 | async-start | bytes 4194304 | tf_op jit(solution)/shard_map/all_to_all | solution.py:74
  101.2 1.6 copy-start.1
  101.2 1.9 copy-start.2
  123.1 1.4 copy-start.7
  124.6 0.8 copy-start.8
  125.4 1.6 copy-start.1
  125.4 1.9 copy-start.2
  147.2 1.4 copy-start.7
  148.7 0.8 copy-start.8
  167.0 60.2 %copy-start.4 = (bf16[64,64,128]{2,1,0:T(8,128)(2,1)S(1)}, bf16[64,64,128]{2,1,0:T(8,128)(2,1)}, u32[]{:S(2)}) copy-start(bf16[64,64,128]{2,1,0:T(8,128)(2,1)} %param.13) | copy-start | bytes 3145732
  167.0 56.3 %all-to-all-start.4 = ((bf16[64,4,2,2,8,128]{5,4,3,2,1,0:T(8,128)(2,1)}), bf16[64,4,2,2,8,128]{5,4,3,2,1,0:T(8,128)(2,1)S(1)}, u32[]{:S(2)}, u32[]{:S(2)}) async-start(bf16[64,4,2,2,8,128]{5,4,3,2,1,0:T(8,128)(2,1)} %bitcast.121), calls=%async_computation.4 | async-start | bytes 4194304 | tf_op jit(solution)/shard_map/all_to_all | solution.py:83
  223.3 8.2 %all-to-all-start.3 = ((f32[4,1,2048]{2,1,0:T(1,128)}), f32[4,1,2048]{2,1,0:T(1,128)}, u32[]{:S(2)}, u32[]{:S(2)}) async-start(f32[4,1,2048]{2,1,0:T(1,128)} %reshape.94), calls=%async_computation.3 | async-start | bytes 65536 | tf_op jit(solution)/shard_map/all_to_all | solution.py:89
  229.6 6.6 %copy-start.13 = (s32[64]{0:T(128)S(1)}, s32[64]{0:T(128)}, u32[]{:S(2)}) copy-start(s32[64]{0:T(128)} %param.15) | copy-start | bytes 772
  231.5 29.3 %all-to-all-start.5 = ((bf16[64,4,2,2,8,128]{5,4,3,2,0,1:T(8,128)(2,1)}), bf16[64,4,2,2,8,128]{5,4,3,2,0,1:T(8,128)(2,1)}, u32[]{:S(2)}, u32[]{:S(2)}) async-start(bf16[64,4,2,2,8,128]{5,4,3,2,0,1:T(8,128)(2,1)} %copy.115), calls=%async_computation.5 | async-start | bytes 4194304 | tf_op jit(solution)/shard_map/all_to_all | solution.py:82
  241.5 2.6 copy-start.10
  241.5 4.1 %copy-start.12 = (s32[64]{0:T(128)S(1)}, s32[64]{0:T(128)}, u32[]{:S(2)}) copy-start(s32[64]{0:T(128)} %copy-done.11) | copy-start | bytes 772
  242.6 5.8 %copy-start.9 = (f32[64,8,1,8]{0,3,1,2:T(8,128)S(1)}, f32[64,8,1,8]{0,3,1,2:T(8,128)}, u32[]{:S(2)}) copy-start(f32[64,8,1,8]{0,3,1,2:T(8,128)} %copy.125) | copy-start | bytes 49156
where the time goes:
time: 275 us; the launch traced here: 273 us
  waiting for transfers between devices  82 us (30%)
  blocking collectives  79.7 us (29%)
  matrix products  37.3 us (14%)
  local copies, waits for them, and re-layouts  35 us (13%)
  other arithmetic  20.7 us (8%)
  starting transfers between devices  18 us (7%)
    all_to_all x1, blocking collectives, body(): lax.all_to_all(outbox, 'prefix', split_axis=0, concat_axis=0, tiled=True)  64 us
    all_to_all x1, waiting for transfers between devices, body(): lax.all_to_all(blended, 'prefix', split_axis=0, concat_axis=0, tiled=True)  46.7 us
    all_to_all x1, waiting for transfers between devices, body(): lax.all_to_all(lax.all_to_all(outbox, 'prefix', split_axis=0, concat_axis...  24.4 us
    all_to_all x1, blocking collectives, body(): lax.all_to_all(log_mass, 'prefix', split_axis=0, concat_axis=0, tiled=True)  15.6 us
    dot_general x8, matrix products, per_group(): jnp.einsum('ncgt,td->ncgd', weights_raw.astype(jnp.bfloat16), head_values...  14.2 us
    reduce_sum x8, other arithmetic, per_group(): totals = jnp.sum(weights_raw, axis=-1)  13.6 us
    dot_general x8, matrix products, per_group(): jnp.einsum('ncgd,td->ncgt', block_query_rows, head_keys, preferred_elemen...  11.4 us
    all_to_all x1, waiting for transfers between devices, body(): lax.all_to_all(lax.all_to_all(blended, 'prefix', split_axis=0, concat_axi...  9.02 us
  transfers between devices with their start and end apart: 4, of which 4 were waited for; matrix products, arithmetic and copies ran while one was open for 9% of the time, Pallas kernels for 0%

commit v1 on v0

v1 whole, which is shorter than its diff:
```python
import functools
import math

import jax
import jax.numpy as jnp
from jax import lax
from jax.experimental import pallas as pl
from jax.experimental.pallas import tpu as pltpu
from jax.sharding import PartitionSpec as P

MESH = pl.DeviceIdType.MESH
BF16 = jnp.bfloat16
F32 = jnp.float32
LOG2E = 1.4426950408889634
CAP = 2
PER_KV = 8
GROUP = 16
KEY_BLOCK = 256
TILE = 256


def axes_of(prefixes):
    return {64: (4, 8, 2)}[prefixes]


def step_offset(i, nz):
    odd = i % 2
    return odd * ((i + 1) // 2) + (1 - odd) * ((nz - i // 2) % nz)


def kernel(
    sizes,
    src_row,
    row_a,
    row_s,
    suf_len,
    arrival,
    q,
    kp_hbm,
    vp_hbm,
    sk_hbm,
    sv_hbm,
    nk,
    nv,
    out,
    out_a,
    in_a,
    in_b,
    out_bp,
    in_bp,
    in_ap,
    out_m,
    in_m,
    in_mp,
    sk,
    sv,
    kf,
    vf,
    stage,
    kc,
    vt,
    scores,
    sacc,
    smass,
    gath,
    pmt,
    load_sem,
    a_send,
    a_recv,
    b_send,
    b_recv,
    bp_send,
    bp_recv,
    m_send,
    m_recv,
    ap_send,
    ap_recv,
    mp_send,
    mp_recv,
):
    nx, nz, nc, ny = sizes
    plane = nx * nc * ny
    rows = q.shape[0]
    width = q.shape[-1]
    keys = kc.shape[0]
    scale = LOG2E / math.sqrt(width)
    me_p, y = lax.axis_index("prefix"), lax.axis_index("head")
    x, z, c = me_p // (nz * nc), (me_p // nc) % nz, me_p % nc

    def at(x_, z_, c_, y_):
        return ((x_ * nz + z_) * nc + c_, y_)

    def along_z(d):
        return at(x, (z + d) % nz, c, y)

    def in_plane(j, sign):
        jx, jc, jy = j // (nc * ny), (j // ny) % nc, j % ny
        return at((x + nx + sign * jx) % nx, z, (c + jc) % nc, (y + ny + sign * jy) % ny)

    loads = [
        pltpu.make_async_copy(s, d, load_sem.at[n])
        for n, (s, d) in enumerate(((kp_hbm, kf), (vp_hbm, vf), (sk_hbm, sk), (sv_hbm, sv)))
    ]
    for load in loads:
        load.start()

    barrier = pltpu.get_barrier_semaphore()

    @pl.loop(1, nz)
    def _(d):
        pl.semaphore_signal(barrier, inc=1, device_id=along_z(d), device_id_type=MESH)

    @pl.loop(1, plane)
    def _(j):
        pl.semaphore_signal(barrier, inc=1, device_id=in_plane(j, 1), device_id_type=MESH)

    def pack(i, dst):
        @pl.loop(0, nx * nc)
        def _(k):
            for s in range(CAP):
                row = src_row[(i * nx * nc + k) * CAP + s]
                for jy in range(ny):
                    dst[i, k * ny + jy, s] = q[row, (y + jy) % ny]

    pack(0, in_a)

    @pl.loop(1, nz)
    def _(i):
        pack(i, out_a)

    pl.semaphore_wait(barrier, nz - 1 + plane - 1)

    def a_copy(i):
        return pltpu.make_async_remote_copy(
            out_a.at[i], in_a.at[i], a_send.at[i], a_recv.at[i],
            device_id=along_z(step_offset(i, nz)), device_id_type=MESH,
        )

    def start_b(i):
        pltpu.make_async_copy(in_a.at[i, 0], in_b.at[i, 0], b_recv.at[i]).start()

        @pl.loop(1, plane)
        def _(j):
            pltpu.make_async_remote_copy(
                in_a.at[i, j], in_b.at[i, j], b_send.at[i], b_recv.at[i],
                device_id=in_plane(j, 1), device_id_type=MESH,
            ).start()

    def start_bp(i):
        pltpu.make_async_copy(out_bp.at[i, 0], in_bp.at[i, 0], bp_recv.at[i]).start()
        pltpu.make_async_copy(out_m.at[i, 0], in_m.at[i, 0], m_recv.at[i]).start()

        @pl.loop(1, plane)
        def _(j):
            pltpu.make_async_remote_copy(
                out_m.at[i, j // 4], in_m.at[i, j], m_send.at[i], m_recv.at[i],
                device_id=in_plane(j, -1), device_id_type=MESH,
            ).start()
            pltpu.make_async_remote_copy(
                out_bp.at[i, j], in_bp.at[i, j], bp_send.at[i], bp_recv.at[i],
                device_id=in_plane(j, -1), device_id_type=MESH,
            ).start()

    def ap_copies(i):
        back = along_z((nz - step_offset(i, nz)) % nz)
        return (
            pltpu.make_async_remote_copy(
                in_m.at[i], in_mp.at[i], mp_send.at[i], mp_recv.at[i],
                device_id=back, device_id_type=MESH,
            ),
            pltpu.make_async_remote_copy(
                in_bp.at[i], in_ap.at[i], ap_send.at[i], ap_recv.at[i],
                device_id=back, device_id_type=MESH,
            ),
        )

    def wait_all(ref, sem):
        pltpu.make_async_copy(ref, ref, sem).wait()

    @pl.loop(1, nz)
    def _(i):
        a_copy(i).start()

    start_b(0)

    loads[0].wait()
    for part in range(2 * keys // 1024):
        stage[part * 1024 : (part + 1) * 1024] = kf[part * 1024 : (part + 1) * 1024].astype(F32)
    for part in range(keys // KEY_BLOCK):
        for k in range(2):
            block = stage[pl.ds(part * 2 * KEY_BLOCK + k, KEY_BLOCK, stride=2), :]
            kc[part * KEY_BLOCK : (part + 1) * KEY_BLOCK, k * width : (k + 1) * width] = block.astype(BF16)
    loads[1].wait()
    for part in range(2 * keys // 1024):
        stage[part * 1024 : (part + 1) * 1024] = vf[part * 1024 : (part + 1) * 1024].astype(F32)
    for part in range(keys // KEY_BLOCK):
        for k in range(2):
            block = stage[pl.ds(part * 2 * KEY_BLOCK + k, KEY_BLOCK, stride=2), :]
            vt[k * width : (k + 1) * width, part * KEY_BLOCK : (part + 1) * KEY_BLOCK] = block.T.astype(BF16)
    loads[2].wait()
    loads[3].wait()

    kv = nk.shape[1]
    cols = sk.shape[1]
    heads = ny * GROUP
    head_of = lax.broadcasted_iota(jnp.int32, (heads, cols), 0) // PER_KV
    col = lax.broadcasted_iota(jnp.int32, (heads, cols), 1)
    own_head = head_of == col % kv

    def suffix_row(r):
        qr = q[r].reshape(heads, width)
        s = lax.dot_general(qr, sk[r], (((1,), (1,)), ((), ())), preferred_element_type=F32)
        s = jnp.where(own_head & (col < suf_len[r] * kv), s * scale, -1e30)
        new_k = jnp.broadcast_to(nk[r].astype(F32)[:, None, :], (kv, PER_KV, width)).reshape(heads, width)
        new_v = jnp.broadcast_to(nv[r].astype(F32)[:, None, :], (kv, PER_KV, width)).reshape(heads, width)
        own = jnp.sum(qr.astype(F32) * new_k, axis=1, keepdims=True) * scale
        top = jnp.maximum(jnp.max(s, axis=1, keepdims=True), own)
        w = jnp.exp2(s - top)
        own_w = jnp.exp2(own - top)
        total = jnp.sum(w, axis=1, keepdims=True) + own_w
        acc = jnp.dot(w.astype(BF16), sv[r], preferred_element_type=F32)
        acc = acc + own_w.astype(BF16).astype(F32) * new_v
        sacc[r] = (acc / total).reshape(ny, GROUP, width)
        smass[r] = jnp.broadcast_to(top + jnp.log2(total), (heads, width)).reshape(ny, GROUP, width)

    part_rows = rows // nz

    def suffix_part(i):
        @pl.loop(0, part_rows // 2)
        def _(n):
            suffix_row(i * part_rows + 2 * n)
            suffix_row(i * part_rows + 2 * n + 1)

    low_row = lax.broadcasted_iota(jnp.int32, (TILE, width), 0) % GROUP < PER_KV
    low_lane = lax.broadcasted_iota(jnp.int32, (width, TILE), 1) % GROUP < PER_KV
    senders = TILE // (CAP * GROUP)

    def attend(i):
        for t in range(plane // senders):
            xq = in_b[i, t * senders : (t + 1) * senders].reshape(TILE, width).astype(F32)
            xq = jnp.concatenate(
                [jnp.where(low_row, xq, 0.0), jnp.where(low_row, 0.0, xq)], axis=1
            ).astype(BF16)
            top = None
            for b in range(keys // KEY_BLOCK):
                part = slice(b * KEY_BLOCK, (b + 1) * KEY_BLOCK)
                s = lax.dot_general(kc[part], xq, (((1,), (1,)), ((), ())), preferred_element_type=F32)
                scores[t % 2, part] = s
                high = jnp.max(s, axis=0, keepdims=True)
                top = high if top is None else jnp.maximum(top, high)
            top = top * scale
            total = jnp.zeros_like(top)
            acc = jnp.zeros((2 * width, TILE), F32)
            for b in range(keys // KEY_BLOCK):
                part = slice(b * KEY_BLOCK, (b + 1) * KEY_BLOCK)
                w = jnp.exp2(scores[t % 2, part] * scale - top)
                total = total + jnp.sum(w, axis=0, keepdims=True)
                acc = acc + jnp.dot(vt[:, part], w.astype(BF16), preferred_element_type=F32)
            o = jnp.where(low_lane, acc[:width], acc[width:]) / total
            out_bp[i, t * senders : (t + 1) * senders] = o.T.astype(BF16).reshape(senders, CAP, GROUP, width)
            mass = top + jnp.log2(total)
            for h in range(TILE // 128):
                out_m[i, t * (TILE // 128) + h] = mass[:, h * 128 : (h + 1) * 128]

    @pl.loop(1, nz + 3)
    def _(n):
        @pl.when(n < nz)
        def _():
            a_copy(n).wait_recv()
            start_b(n)

        @pl.when(n <= nz)
        def _():
            i = n - 1
            suffix_part(i)
            wait_all(in_b.at[i], b_recv.at[i])
            attend(i)
            start_bp(i)

        @pl.when((n >= 2) & (n < nz + 2))
        def _():
            i = n - 2
            wait_all(in_bp.at[i], bp_recv.at[i])
            wait_all(in_m.at[i], m_recv.at[i])

            @pl.when(i > 0)
            def _():
                for copy in ap_copies(i):
                    copy.start()

            @pl.when(i == 0)
            def _():
                pltpu.make_async_copy(in_m.at[0], in_mp.at[0], mp_recv.at[0]).start()
                pltpu.make_async_copy(in_bp.at[0], in_ap.at[0], ap_recv.at[0]).start()

    wait_all(in_b.at[0, pl.ds(1, plane - 1)], b_send.at[0])
    wait_all(in_bp.at[0, pl.ds(1, plane - 1)], bp_send.at[0])
    wait_all(in_m.at[0, pl.ds(1, plane - 1)], m_send.at[0])
    wait_all(in_mp.at[0], mp_recv.at[0])
    wait_all(in_ap.at[0], ap_recv.at[0])

    @pl.loop(1, nz)
    def _(i):
        a_copy(i).wait_send()
        wait_all(in_b.at[i, pl.ds(1, plane - 1)], b_send.at[i])
        wait_all(in_bp.at[i, pl.ds(1, plane - 1)], bp_send.at[i])
        wait_all(in_m.at[i, pl.ds(1, plane - 1)], m_send.at[i])
        for copy in ap_copies(i):
            copy.wait()

    @pl.loop(0, rows)
    def _(r):
        a = row_a[r]
        i, k = a // (nx * nc), a % (nx * nc)
        for jy in range(ny):
            gath[jy, pl.ds(r, 1), :] = in_mp[i, k * ny + jy]

    for jy in range(ny):
        turned = gath[jy].T
        first = turned[(jy % 4) * 32 : (jy % 4) * 32 + GROUP]
        second = turned[(jy % 4) * 32 + GROUP : (jy % 4) * 32 + 2 * GROUP]
        pmt[jy] = jnp.where(arrival[...] == 0, first, second)

    lane = lax.broadcasted_iota(jnp.int32, (GROUP, rows), 1)

    def merge_row(r):
        a, s = row_a[r], row_s[r]
        i, k = a // (nx * nc), a % (nx * nc)
        for jy in range(ny):
            yy = (y + jy) % ny
            pm = jnp.sum(jnp.where(lane == r, pmt[jy], 0.0), axis=1, keepdims=True)
            gap = smass[r, yy] - pm
            e = jnp.exp2(-jnp.abs(gap))
            ahead = gap <= 0
            po = in_ap[i, k * ny + jy, s].astype(F32)
            so = sacc[r, yy]
            merged = (jnp.where(ahead, 1.0, e) * po + jnp.where(ahead, e, 1.0) * so) / (1.0 + e)
            out[r, yy] = merged.astype(BF16)

    @pl.loop(0, rows // 2)
    def _(n):
        merge_row(2 * n)
        merge_row(2 * n + 1)


def body(
    queries,
    prefix_id,
    suffix_len,
    prefix_keys,
    prefix_values,
    suffix_keys,
    suffix_values,
    new_keys,
    new_values,
):
    rows, heads, width = queries.shape
    prefixes, ny = lax.axis_size("prefix"), lax.axis_size("head")
    nx, nz, nc = axes_of(prefixes)
    plane = nx * nc * ny
    keys = prefix_keys.shape[1]
    slots, kv = suffix_keys.shape[1:3]

    me_p = lax.axis_index("prefix")
    x, z, c = me_p // (nz * nc), (me_p // nc) % nz, me_p % nc
    target = prefix_id[:, 0]
    dz = (target // nc - z) % nz
    step = jnp.where(dz == 0, 0, jnp.where(2 * dz <= nz, 2 * dz - 1, 2 * (nz - dz)))
    row_a = (step * nx + (target // (nz * nc) - x) % nx) * nc + (target - c) % nc
    r_index = lax.broadcasted_iota(jnp.int32, (rows, rows), 0)
    c_index = lax.broadcasted_iota(jnp.int32, (rows, rows), 1)
    same = (target[None, :] == target[:, None]) & (c_index < r_index)
    arrival = jnp.sum(same.astype(jnp.int32), axis=1)
    place = row_a * CAP + arrival
    slot_index = lax.broadcasted_iota(jnp.int32, (prefixes * CAP, rows), 0)
    row_index = lax.broadcasted_iota(jnp.int32, (prefixes * CAP, rows), 1)
    src_row = jnp.sum(jnp.where(place[None, :] == slot_index, row_index, 0), axis=1)

    smem = pl.BlockSpec(memory_space=pltpu.SMEM)
    vmem = pl.BlockSpec(memory_space=pltpu.VMEM)
    hbm = pl.BlockSpec(memory_space=pl.ANY)
    message = (CAP, GROUP, width)
    dma = pltpu.SemaphoreType.DMA
    attended = pl.pallas_call(
        functools.partial(kernel, (nx, nz, nc, ny)),
        out_shape=jax.ShapeDtypeStruct((rows, ny, GROUP, width), BF16),
        in_specs=[smem] * 4 + [vmem] * 2 + [hbm] * 4 + [vmem] * 2,
        out_specs=vmem,
        scratch_shapes=[
            pltpu.VMEM((nz, plane) + message, BF16),
            pltpu.VMEM((nz, plane) + message, BF16),
            pltpu.VMEM((nz, plane) + message, BF16),
            pltpu.VMEM((nz, plane) + message, BF16),
            pltpu.VMEM((nz, plane) + message, BF16),
            pltpu.VMEM((nz, plane) + message, BF16),
            pltpu.VMEM((nz, plane // 4, 1, 128), F32),
            pltpu.VMEM((nz, plane, 1, 128), F32),
            pltpu.VMEM((nz, plane, 1, 128), F32),
            pltpu.VMEM((rows, slots * kv, width), BF16),
            pltpu.VMEM((rows, slots * kv, width), BF16),
            pltpu.VMEM((2 * keys, width), BF16),
            pltpu.VMEM((2 * keys, width), BF16),
            pltpu.VMEM((2 * keys, width), F32),
            pltpu.VMEM((keys, 2 * width), BF16),
            pltpu.VMEM((2 * width, keys), BF16),
            pltpu.VMEM((2, keys, TILE), F32),
            pltpu.VMEM((rows, ny, GROUP, width), F32),
            pltpu.VMEM((rows, ny, GROUP, width), F32),
            pltpu.VMEM((ny, rows, 128), F32),
            pltpu.VMEM((ny, GROUP, rows), F32),
            dma((4,)),
        ]
        + [dma((nz,))] * 12,
        compiler_params=pltpu.CompilerParams(
            collective_id=0, has_side_effects=True, vmem_limit_bytes=56 * 2**20
        ),
    )(
        src_row,
        row_a,
        arrival,
        suffix_len,
        arrival[None, :],
        queries.reshape(rows, ny, GROUP, width),
        prefix_keys.reshape(2 * keys, width),
        prefix_values.reshape(2 * keys, width),
        suffix_keys.reshape(rows, slots * kv, width),
        suffix_values.reshape(rows, slots * kv, width),
        new_keys,
        new_values,
    )
    return attended.reshape(rows, heads, width)


def solution(mesh):
    rows = P(("prefix", "head"))
    cache = P("prefix", None, "head", None)
    return jax.shard_map(
        body,
        mesh=mesh,
        in_specs=(rows, rows, rows, cache, cache, rows, rows, rows, rows),
        out_specs=rows,
        check_vma=False,
    )
```

time: 275 us -> 133 us (0.48)
  Pallas kernels: 0 us -> 127 us
  waiting for transfers between devices: 82 us -> 0 us
  blocking collectives: 79.7 us -> 0 us
  matrix products: 37.3 us -> 0 us
  local copies, waits for them, and re-layouts: 35 us -> 2.27 us
  starting transfers between devices: 18 us -> 0 us
  other arithmetic: 20.7 us -> 2.78 us
    pallas_call x0 -> x1, Pallas kernels: none -> 127 us  [body(): pl.pallas_call(functools.partial(kernel, (nx, nz, nc, ny)), out_shape=jax...]
    all_to_all x4 -> x0, waiting for transfers between devices: 82 us -> none  [the longest x1 46.7 us: body(): lax.all_to_all(blended, 'prefix', split_axis=0, concat_axis=0, tiled=True)]
    all_to_all x2 -> x0, blocking collectives: 79.7 us -> none  [the longest x1 64 us: body(): lax.all_to_all(outbox, 'prefix', split_axis=0, concat_axis=0, tiled=True)]
    dot_general x19 -> x0, matrix products: 37.3 us -> none  [the longest x8 14.2 us: per_group(): jnp.einsum('ncgt,td->ncgd', weights_raw.astype(jnp.bfloat16), head_values...]
    all_to_all x4 -> x0, starting transfers between devices: 18 us -> none  [the longest x1 4.92 us: body(): lax.all_to_all(blended, 'prefix', split_axis=0, concat_axis=0, tiled=True)]
    reduce_sum x10 -> x2, other arithmetic: 15.9 us -> 1.59 us  [the longest x1 0.91 us: body(): arrival = jnp.sum(same.astype(jnp.int32), axis=1)]
    all_to_all x7 -> x0, local copies, waits for them, and re-layouts: 9.13 us -> none  [the longest x1 3.53 us: body(): lax.all_to_all(lax.all_to_all(blended, 'prefix', split_axis=0, concat_axi...]
    squeeze x4 -> x0, local copies, waits for them, and re-layouts: 3.25 us -> none  [attend(): lax.map(per_head, (lined, jnp.transpose(key_cache, (1, 0, 2)), jnp.transp...]
  transfers between devices with their start and end apart: 4 -> 0, of which waited for: 4 -> 0; matrix products, arithmetic and copies ran while one was open for 9% -> 0% of each run, Pallas kernels for 0% -> 0%
where the time goes in v1:
time: 133 us; the launch traced here: 132 us
  Pallas kernels  127 us (95%)
  other arithmetic  2.78 us (2%)
  local copies, waits for them, and re-layouts  2.27 us (2%)
    pallas_call x1, Pallas kernels, body(): pl.pallas_call(functools.partial(kernel, (nx, nz, nc, ny)), out_shape=jax...  127 us

profile of v1, /device:TPU:1, one launch (start us, length us, event | category | flops | bytes accessed | tf_op | source)
XLA Modules:
  0.0 131.7 jit_solution(10061317586614201265)
XLA Ops:
  0.0 0.9 convert_reduce_fusion.row_s
  0.9 0.0 copy-start
  0.9 1.2 multiply_add_fusion
  2.1 0.7 select_reduce_fusion.src_row
  2.8 0.0 copy-done
  2.8 126.6 %shard_map.91 = bf16[64,4,16,128]{3,2,1,0:T(8,128)(2,1)} custom-call(s32[128]{0:T(128)} %select_reduce_fusion.src_row, s32[64]{0:T(128)} %get-tuple-element.6.row_a, s32[64]{0:T(128)} %copy-done, s32[64]{0:T(128)} %suf_len.1, s32[1,64]{1,0:T(1,128)} %bitcast.16, bf16[64,4,16,128]{3,2,1,0:T(8,128)(2,1)} %bitcast.13, bf16[4096,128]{1,0:T(8,128)(2,1)} %bitcast.14, ...), custom_call_target="tpu_custom_call" | custom-call | tf_op jit(solution)/shard_map/pallas_call | solution.py:384
  129.4 2.3 %copy.11 = bf16[64,64,128]{2,1,0:T(8,128)(2,1)} copy(bf16[64,64,128]{2,1,0:T(8,128)(2,1)} %bitcast.12) | data formatting | bytes 2097152
Async XLA Ops:
  0.9 1.9 %copy-start = (s32[64]{0:T(128)}, s32[64]{0:T(128)S(1)}, u32[]{:S(2)}) copy-start(s32[64]{0:T(128)S(1)} %convert_reduce_fusion.row_s) | copy-start | bytes 772
